TPU v7x, 32 devices: a whole 2x2x4 slice. The times are simulated.
32 devices in a mesh: sec: 4 (over y, x), row: 8 (over z, core).
Axes of the slice: x: 2, y: 2, z: 4, core: 2. Of those that a mesh axis runs over, the one named last changes fastest.
Arguments:
- rhs: float32 [4096, 256], P(('sec', 'row')), may hold values from -6 to 6
- coupling: bfloat16 [4, 1024, 4096], P(None, 'row', 'sec'), may hold values from -0.09375 to 0.09375
- diag_inverse: bfloat16 [4, 1024, 1024], P('sec'), as said below
Outputs:
- solution: float32 [4096, 256], P(('sec', 'row'))
- forward: float32 [4096, 256], P(('sec', 'row'))
Inputs may be any that keep to these rules, and one draw needn't show every extreme that they name: `diag_inverse`: each of the 4 blocks is lower triangular with diagonal entries from 0.5 to 1.5.
All inputs are finite; a program needn't handle non-finite values.
Results may differ from a plain program's by a relative error of at most 0.02.
Values may be sent and summed in bfloat16 or wider, within the bound.
A program may use at most 64 MiB of HBM per device.

v0:
```python
import jax
import jax.numpy as jnp
from jax import lax
from jax.sharding import PartitionSpec as P


def from_behind(x, axis, by):
    devices = lax.axis_size(axis)
    pairs = [(i, i + by) for i in range(devices) if 0 <= i + by < devices]
    return lax.ppermute(x, axis, pairs)


def local(rhs, coupling, diag_inverse):
    sections = lax.axis_size("sec")
    me_sec = lax.axis_index("sec")
    me_row = lax.axis_index("row")
    inverse = diag_inverse[0]
    rows, total = rhs.shape
    width = inverse.shape[0]
    groups = 1
    cols = total // groups
    ticks = sections + groups - 1
    flat_coupling = coupling.reshape(sections * rows, width)
    later_mask = (jnp.arange(sections) > me_sec)[:, None, None]

    def forward_tick(tick, carry):
        kept, passing = carry
        group = tick - me_sec
        active = (group >= 0) & (group < groups)
        arrived = lax.dynamic_index_in_dim(passing, me_sec, 0, keepdims=False)
        resid = (rhs - arrived).astype(jnp.bfloat16)
        whole = lax.all_gather(resid, "row", axis=0, tiled=True)

        def forward_solve_block():
            solved = jnp.dot(inverse, whole, preferred_element_type=jnp.float32)
            update = jnp.dot(
                flat_coupling, solved.astype(jnp.bfloat16), preferred_element_type=jnp.float32
            )
            return (solved, update.reshape(sections, rows, cols))

        def forward_skip_block():
            return (
                jnp.zeros((width, cols), jnp.float32),
                jnp.zeros((sections, rows, cols), jnp.float32),
            )

        solved, update = lax.cond(active, forward_solve_block, forward_skip_block)
        outgoing = passing + jnp.where(later_mask, update, 0.0)
        kept = jnp.where(active, solved, kept)
        passing = from_behind(outgoing.astype(jnp.bfloat16), "sec", 1).astype(outgoing.dtype)
        return (kept, passing)

    kept = jnp.zeros((width, total), jnp.float32)
    passing = jnp.zeros((sections, rows, cols), jnp.float32)
    kept, passing = lax.fori_loop(0, ticks, forward_tick, (kept, passing))

    def backward_tick(tick, carry):
        solution, partial_value, arrived = carry

        def add_source(group_now, partial_now):
            source = group_now - tick + sections
            valid = (source > me_sec) & (source < sections)
            safe = jnp.clip(source, 0, sections - 1).astype(jnp.int32)
            block = lax.dynamic_index_in_dim(coupling, safe, 0, keepdims=False)
            incoming = lax.dynamic_index_in_dim(arrived, safe, 0, keepdims=False)

            def compute_term():
                return lax.dot_general(
                    block, incoming, (((0,), (0,)), ((), ())), preferred_element_type=jnp.float32
                )

            def skip_term():
                return jnp.zeros((width, cols), jnp.float32)

            term = lax.cond(valid, compute_term, skip_term)
            return partial_now + term

        partial_value = lax.fori_loop(0, groups, add_source, partial_value)
        group = tick - (sections - 1 - me_sec)
        active = (group >= 0) & (group < groups)
        summed = lax.psum(partial_value.astype(jnp.bfloat16), "row").astype(jnp.float32)
        forward_part = kept

        def backward_solve_block():
            lowered = (forward_part - summed).astype(jnp.bfloat16)
            return lax.dot_general(
                inverse, lowered, (((0,), (0,)), ((), ())), preferred_element_type=jnp.float32
            )

        def backward_skip_block():
            return jnp.zeros((width, cols), jnp.float32)

        solved = lax.cond(active, backward_solve_block, backward_skip_block)
        solved_rows = lax.dynamic_slice_in_dim(solved, me_row * rows, rows, 0)
        solution = jnp.where(active, solved_rows, solution)
        gathered = lax.all_gather(solved_rows.astype(jnp.bfloat16), "sec", axis=0, tiled=True)
        arrived = gathered.reshape(sections, rows, cols)
        return (solution, partial_value, arrived)

    solution = jnp.zeros((rows, total), jnp.float32)
    partial_value = jnp.zeros((width, total), jnp.float32)
    arrived = jnp.zeros((sections, rows, cols), jnp.bfloat16)
    solution, partial_value, arrived = lax.fori_loop(
        0, ticks, backward_tick, (solution, partial_value, arrived)
    )
    forward_rows = lax.dynamic_slice_in_dim(kept, me_row * rows, rows, 0)
    return (solution, forward_rows)


def solution(mesh):
    return jax.shard_map(
        local,
        mesh=mesh,
        in_specs=(P(("sec", "row"), None), P(None, "row", "sec"), P("sec", None, None)),
        out_specs=(P(("sec", "row"), None), P(("sec", "row"), None)),
        check_vma=False,
    )
```

profile of v0, /device:TPU:0, one launch (start us, length us, event | category | flops | bytes accessed | tf_op | source)
XLA Modules:
  0.0 420.8 jit_solution(6176833018257158925)
XLA Ops:
  7.2 120.7 %while.50 = (s32[]{:T(128)}, f32[1024,256]{1,0:T(8,128)S(1)}, f32[4,128,256]{2,1,0:T(8,128)S(1)}, s32[]{:T(128)}, s32[]{:T(128)}, /*index=5*/f32[128,256]{1,0:T(...) while((s32[]{:T(128)}, f32[1024,256]{1,0:T(8,128)S(1)}, ...), condition=%wide.region_3.4_spmd.clone.clone.clone, body=%wide.region_0.3_spmd.clone.clone.clone.sunk | while | flops 806944768 | bytes 19792148 | solution.py:55
  7.3 0.9 fusion.19
  8.2 16.6 %all_gather.25 = bf16[1024,256]{1,0:T(8,128)(2,1)S(1)} all-gather(bf16[128,256]{1,0:T(8,128)(2,1)S(1)} %fusion.19), channel_id=1, replica_groups=mesh['sec'=4,'row'=8] {'row'}, dimensions={0}, use_global_device_ids=true | all-gather | bytes 589824 | tf_op jit(solution)/shard_map/while/body/eval_jaxpr/all_gather | solution.py:32
  24.8 5.3 %conditional.13 = (f32[1024,256]{1,0:T(8,128)}, f32[4,128,256]{2,1,0:T(8,128)S(1)}) conditional(s32[]{:T(128)} %convert_element_type.126, () %tuple.145, (bf16[1024,1024]{1,0:T(8,128)(2,1)}, bf16[1024,256]{1,0:T(8,128)(2,1)S(1)}, bf16[512,1024]{1,0:T(8,128)(2,1)}) %tuple.146), branch_computations={%region_1.1_spmd, %region_2.2_spmd} | conditional | flops 805568512 | bytes 11534380 | solution.py:47
  24.8 3.4 fusion.11
  28.2 1.7 convolution_bitcast_fusion
  30.2 1.3 collective-permute-start
  31.5 1.5 select_select_fusion.5
  33.0 4.8 %collective-permute-done = bf16[4,128,256]{2,1,0:T(8,128)(2,1)S(1)} collective-permute-done((bf16[4,128,256]{2,1,0:T(8,128)(2,1)S(1)}, bf16[4,128,256]{2,1,0:T(8,128)(2,1)S(1)}, u32[]{:S(2)}, u32[]{:S(2)}) %collective-permute-start) | collective-permute-done | bytes 262176 | tf_op jit(solution)/shard_map/while/body/eval_jaxpr/ppermute | solution.py:10
  38.0 0.9 fusion.19
  38.9 14.9 %all_gather.25 = bf16[1024,256]{1,0:T(8,128)(2,1)S(1)} all-gather(bf16[128,256]{1,0:T(8,128)(2,1)S(1)} %fusion.19), channel_id=1, replica_groups=mesh['sec'=4,'row'=8] {'row'}, dimensions={0}, use_global_device_ids=true | all-gather | bytes 589824 | tf_op jit(solution)/shard_map/while/body/eval_jaxpr/all_gather | solution.py:32
  53.8 1.1 conditional.13
  53.8 1.0 broadcast.19
  55.0 8.6 %collective-permute-start = (bf16[4,128,256]{2,1,0:T(8,128)(2,1)S(1)}, bf16[4,128,256]{2,1,0:T(8,128)(2,1)S(1)}, u32[]{:S(2)}, u32[]{:S(2)}) collective-permute-start(bf16[4,128,256]{2,1,0:T(8,128)(2,1)S(1)} %add_convert_fusion.2), channel_id=1, source_target_pairs={{0,8},{8,16},{16,24},{1,9},{9,17},{17,25},{2,10},{10,18},{18,26},{... | collective-permute-start | bytes 786440 | tf_op jit(solution)/shard_map/while/body/eval_jaxpr/ppermute | solution.py:10
  63.9 5.7 %collective-permute-done = bf16[4,128,256]{2,1,0:T(8,128)(2,1)S(1)} collective-permute-done((bf16[4,128,256]{2,1,0:T(8,128)(2,1)S(1)}, bf16[4,128,256]{2,1,0:T(8,128)(2,1)S(1)}, u32[]{:S(2)}, u32[]{:S(2)}) %collective-permute-start) | collective-permute-done | bytes 262176 | tf_op jit(solution)/shard_map/while/body/eval_jaxpr/ppermute | solution.py:10
  69.8 0.9 fusion.19
  70.7 14.9 %all_gather.25 = bf16[1024,256]{1,0:T(8,128)(2,1)S(1)} all-gather(bf16[128,256]{1,0:T(8,128)(2,1)S(1)} %fusion.19), channel_id=1, replica_groups=mesh['sec'=4,'row'=8] {'row'}, dimensions={0}, use_global_device_ids=true | all-gather | bytes 589824 | tf_op jit(solution)/shard_map/while/body/eval_jaxpr/all_gather | solution.py:32
  85.6 1.1 conditional.13
  85.6 1.0 broadcast.19
  86.8 4.4 %collective-permute-start = (bf16[4,128,256]{2,1,0:T(8,128)(2,1)S(1)}, bf16[4,128,256]{2,1,0:T(8,128)(2,1)S(1)}, u32[]{:S(2)}, u32[]{:S(2)}) collective-permute-start(bf16[4,128,256]{2,1,0:T(8,128)(2,1)S(1)} %add_convert_fusion.2), channel_id=1, source_target_pairs={{0,8},{8,16},{16,24},{1,9},{9,17},{17,25},{2,10},{10,18},{18,26},{... | collective-permute-start | bytes 786440 | tf_op jit(solution)/shard_map/while/body/eval_jaxpr/ppermute | solution.py:10
  91.5 5.7 %collective-permute-done = bf16[4,128,256]{2,1,0:T(8,128)(2,1)S(1)} collective-permute-done((bf16[4,128,256]{2,1,0:T(8,128)(2,1)S(1)}, bf16[4,128,256]{2,1,0:T(8,128)(2,1)S(1)}, u32[]{:S(2)}, u32[]{:S(2)}) %collective-permute-start) | collective-permute-done | bytes 262176 | tf_op jit(solution)/shard_map/while/body/eval_jaxpr/ppermute | solution.py:10
  97.4 0.9 fusion.19
  98.3 15.0 %all_gather.25 = bf16[1024,256]{1,0:T(8,128)(2,1)S(1)} all-gather(bf16[128,256]{1,0:T(8,128)(2,1)S(1)} %fusion.19), channel_id=1, replica_groups=mesh['sec'=4,'row'=8] {'row'}, dimensions={0}, use_global_device_ids=true | all-gather | bytes 589824 | tf_op jit(solution)/shard_map/while/body/eval_jaxpr/all_gather | solution.py:32
  113.3 1.1 conditional.13
  113.3 1.0 broadcast.19
  114.5 7.3 %collective-permute-start = (bf16[4,128,256]{2,1,0:T(8,128)(2,1)S(1)}, bf16[4,128,256]{2,1,0:T(8,128)(2,1)S(1)}, u32[]{:S(2)}, u32[]{:S(2)}) collective-permute-start(bf16[4,128,256]{2,1,0:T(8,128)(2,1)S(1)} %add_convert_fusion.2), channel_id=1, source_target_pairs={{0,8},{8,16},{16,24},{1,9},{9,17},{17,25},{2,10},{10,18},{18,26},{... | collective-permute-start | bytes 786440 | tf_op jit(solution)/shard_map/while/body/eval_jaxpr/ppermute | solution.py:10
  122.1 5.7 %collective-permute-done = bf16[4,128,256]{2,1,0:T(8,128)(2,1)S(1)} collective-permute-done((bf16[4,128,256]{2,1,0:T(8,128)(2,1)S(1)}, bf16[4,128,256]{2,1,0:T(8,128)(2,1)S(1)}, u32[]{:S(2)}, u32[]{:S(2)}) %collective-permute-start) | collective-permute-done | bytes 262176 | tf_op jit(solution)/shard_map/while/body/eval_jaxpr/ppermute | solution.py:10
  128.0 284.8 %while.49 = (s32[]{:T(128)}, f32[128,256]{0,1:T(8,128)S(1)}, f32[1024,256]{1,0:T(8,128)}, bf16[4,128,256]{1,0,2:T(4,128)(2,1)S(1)}, s32[]{:T(128)}, /*index=5*/s...) while((s32[]{:T(128)}, f32[128,256]{0,1:T(8,128)S(1)}, ...), condition=%wide.region_10.11_spmd.clone, body=%wide.region_4.10_spmd.clone.sunk | while | flops 605880320 | bytes 14812509 | solution.py:103
  128.2 1.3 fusion.18
  129.5 64.1 %all-reduce.2.cloned.1.call-done = bf16[1024,256]{1,0:T(8,128)(2,1)} async-done(((bf16[1024,256]{1,0:T(8,128)(2,1)}), bf16[1024,256]{1,0:T(8,128)(2,1)}) %all-reduce.2.cloned.1.call-update) | async-done | bytes 524304 | tf_op jit(solution)/shard_map/while/body/eval_jaxpr/psum | solution.py:81
  193.9 11.0 %all_gather.24 = bf16[512,256]{0,1:T(8,128)(2,1)S(1)} all-gather(bf16[128,256]{0,1:T(8,128)(2,1)S(1)} %dynamic-slice_convert_fusion.2), channel_id=1, replica_groups=mesh['sec'=4,'row'=8] {'sec'}, dimensions={0}, use_global_device_ids=true | all-gather | bytes 327680 | tf_op jit(solution)/shard_map/while/body/eval_jaxpr/all_gather | solution.py:96
  205.0 1.5 conditional.11
  205.2 1.3 fusion.3
  206.5 2.5 fusion.18
  209.1 54.9 %all-reduce.2.cloned.1.call-done = bf16[1024,256]{1,0:T(8,128)(2,1)} async-done(((bf16[1024,256]{1,0:T(8,128)(2,1)}), bf16[1024,256]{1,0:T(8,128)(2,1)}) %all-reduce.2.cloned.1.call-update) | async-done | bytes 524304 | tf_op jit(solution)/shard_map/while/body/eval_jaxpr/psum | solution.py:81
  264.1 11.3 %all_gather.24 = bf16[512,256]{0,1:T(8,128)(2,1)S(1)} all-gather(bf16[128,256]{0,1:T(8,128)(2,1)S(1)} %dynamic-slice_convert_fusion.2), channel_id=1, replica_groups=mesh['sec'=4,'row'=8] {'sec'}, dimensions={0}, use_global_device_ids=true | all-gather | bytes 327680 | tf_op jit(solution)/shard_map/while/body/eval_jaxpr/all_gather | solution.py:96
  275.6 1.5 conditional.11
  275.8 1.3 fusion.3
  277.1 2.5 fusion.18
  279.7 53.5 %all-reduce.2.cloned.1.call-done = bf16[1024,256]{1,0:T(8,128)(2,1)} async-done(((bf16[1024,256]{1,0:T(8,128)(2,1)}), bf16[1024,256]{1,0:T(8,128)(2,1)}) %all-reduce.2.cloned.1.call-update) | async-done | bytes 524304 | tf_op jit(solution)/shard_map/while/body/eval_jaxpr/psum | solution.py:81
  333.4 11.3 %all_gather.24 = bf16[512,256]{0,1:T(8,128)(2,1)S(1)} all-gather(bf16[128,256]{0,1:T(8,128)(2,1)S(1)} %dynamic-slice_convert_fusion.2), channel_id=1, replica_groups=mesh['sec'=4,'row'=8] {'sec'}, dimensions={0}, use_global_device_ids=true | all-gather | bytes 327680 | tf_op jit(solution)/shard_map/while/body/eval_jaxpr/all_gather | solution.py:96
  344.9 1.5 conditional.11
  345.1 1.3 fusion.3
  346.4 2.5 fusion.18
  348.9 53.5 %all-reduce.2.cloned.1.call-done = bf16[1024,256]{1,0:T(8,128)(2,1)} async-done(((bf16[1024,256]{1,0:T(8,128)(2,1)}), bf16[1024,256]{1,0:T(8,128)(2,1)}) %all-reduce.2.cloned.1.call-update) | async-done | bytes 524304 | tf_op jit(solution)/shard_map/while/body/eval_jaxpr/psum | solution.py:81
  402.4 2.5 conditional.12
  402.4 2.5 convolution_bitcast_fusion.1
  405.0 7.7 %all_gather.24 = bf16[512,256]{0,1:T(8,128)(2,1)S(1)} all-gather(bf16[128,256]{0,1:T(8,128)(2,1)S(1)} %dynamic-slice_convert_fusion.2), channel_id=1, replica_groups=mesh['sec'=4,'row'=8] {'sec'}, dimensions={0}, use_global_device_ids=true | all-gather | bytes 327680 | tf_op jit(solution)/shard_map/while/body/eval_jaxpr/all_gather | solution.py:96
  (63 shorter events, 5.6 us)
Async XLA Ops:
  24.8 3.4 copy-start
  30.2 7.6 %collective-permute-start = (bf16[4,128,256]{2,1,0:T(8,128)(2,1)S(1)}, bf16[4,128,256]{2,1,0:T(8,128)(2,1)S(1)}, u32[]{:S(2)}, u32[]{:S(2)}) collective-permute-start(bf16[4,128,256]{2,1,0:T(8,128)(2,1)S(1)} %add_convert_fusion.2), channel_id=1, source_target_pairs={{0,8},{8,16},{16,24},{1,9},{9,17},{17,25},{2,10},{10,18},{18,26},{... | collective-permute-start | bytes 786440 | tf_op jit(solution)/shard_map/while/body/eval_jaxpr/ppermute | solution.py:10
  55.0 14.6 %collective-permute-start = (bf16[4,128,256]{2,1,0:T(8,128)(2,1)S(1)}, bf16[4,128,256]{2,1,0:T(8,128)(2,1)S(1)}, u32[]{:S(2)}, u32[]{:S(2)}) collective-permute-start(bf16[4,128,256]{2,1,0:T(8,128)(2,1)S(1)} %add_convert_fusion.2), channel_id=1, source_target_pairs={{0,8},{8,16},{16,24},{1,9},{9,17},{17,25},{2,10},{10,18},{18,26},{... | collective-permute-start | bytes 786440 | tf_op jit(solution)/shard_map/while/body/eval_jaxpr/ppermute | solution.py:10
  86.8 10.5 %collective-permute-start = (bf16[4,128,256]{2,1,0:T(8,128)(2,1)S(1)}, bf16[4,128,256]{2,1,0:T(8,128)(2,1)S(1)}, u32[]{:S(2)}, u32[]{:S(2)}) collective-permute-start(bf16[4,128,256]{2,1,0:T(8,128)(2,1)S(1)} %add_convert_fusion.2), channel_id=1, source_target_pairs={{0,8},{8,16},{16,24},{1,9},{9,17},{17,25},{2,10},{10,18},{18,26},{... | collective-permute-start | bytes 786440 | tf_op jit(solution)/shard_map/while/body/eval_jaxpr/ppermute | solution.py:10
  114.5 13.4 %collective-permute-start = (bf16[4,128,256]{2,1,0:T(8,128)(2,1)S(1)}, bf16[4,128,256]{2,1,0:T(8,128)(2,1)S(1)}, u32[]{:S(2)}, u32[]{:S(2)}) collective-permute-start(bf16[4,128,256]{2,1,0:T(8,128)(2,1)S(1)} %add_convert_fusion.2), channel_id=1, source_target_pairs={{0,8},{8,16},{16,24},{1,9},{9,17},{17,25},{2,10},{10,18},{18,26},{... | collective-permute-start | bytes 786440 | tf_op jit(solution)/shard_map/while/body/eval_jaxpr/ppermute | solution.py:10
  128.0 65.6 %all-reduce.2.cloned.1.call-start = ((), (), s32[]{:S(2)}) async-start(), calls=%async_computation | async-start | bytes 1048576 | tf_op jit(solution)/shard_map/while/body/eval_jaxpr/psum | solution.py:81
  204.9 59.0 %all-reduce.2.cloned.1.call-start = ((), (), s32[]{:S(2)}) async-start(), calls=%async_computation | async-start | bytes 1048576 | tf_op jit(solution)/shard_map/while/body/eval_jaxpr/psum | solution.py:81
  275.6 57.6 %all-reduce.2.cloned.1.call-start = ((), (), s32[]{:S(2)}) async-start(), calls=%async_computation | async-start | bytes 1048576 | tf_op jit(solution)/shard_map/while/body/eval_jaxpr/psum | solution.py:81
  344.8 57.6 %all-reduce.2.cloned.1.call-start = ((), (), s32[]{:S(2)}) async-start(), calls=%async_computation | async-start | bytes 1048576 | tf_op jit(solution)/shard_map/while/body/eval_jaxpr/psum | solution.py:81
Sparse Core Ops, SparseCore 0:
  131.2 62.4 all-reduce.1
  209.2 54.6 all-reduce.1
  279.8 53.3 all-reduce.1
  349.0 53.3 all-reduce.1
where the time goes:
time: 421 us
  waiting for transfers between devices  248 us (59%)
  blocking collectives  103 us (24%)
  starting transfers between devices  21.8 us (5%)
  other arithmetic  16 us (4%)
  between operations  13.8 us (3%)
  matrix products  11.4 us (3%)
  local copies, waits for them, and re-layouts  6.19 us (1%)
    psum x4, waiting for transfers between devices, backward_tick(): lax.psum(partial_value.astype(jnp.bfloat16), 'row').astype(jnp.float32)  226 us
    all_gather x4, blocking collectives, forward_tick(): whole = lax.all_gather(resid, 'row', axis=0, tiled=True)  61.3 us
    all_gather x4, blocking collectives, backward_tick(): lax.all_gather(solved_rows.astype(jnp.bfloat16), 'sec', axis=0, tiled=True)  41.4 us
    ppermute x4, waiting for transfers between devices, from_behind(): return lax.ppermute(x, axis, pairs)  22.1 us
    ppermute x4, starting transfers between devices, from_behind(): return lax.ppermute(x, axis, pairs)  21.6 us
    convert_element_type x4, other arithmetic, backward_tick(): partial_value.astype(jnp.bfloat16)  8.93 us
  transfers between devices with their start and end apart: 8, of which 8 were waited for; matrix products, arithmetic and copies ran while one was open for 1% of the time, Pallas kernels for 0%

commit v1 on v0

v1 whole, which is shorter than its diff:
```python
import functools

import jax
import jax.numpy as jnp
from jax import lax
from jax.experimental import pallas as pl
from jax.experimental.pallas import tpu as pltpu
from jax.sharding import PartitionSpec as P

MESH = pl.DeviceIdType.MESH
F32 = jnp.float32
BF16 = jnp.bfloat16
GROUPS = 4


def nt(a, b):
    return lax.dot_general(a, b, (((1,), (1,)), ((), ())), preferred_element_type=F32)


def nn(a, b):
    return jnp.dot(a, b, preferred_element_type=F32)


def kernel(S, R, G, rhs, coup, D, sol, fwd,
           E, rT, rTl, rb, res, mco, pas, pso, yb, fs, fb, dto, dti, xs, rso, rsi, rli, sob, soi,
           e_s, e_r, rh_s, rh_r, a0_s, a0_r, mc_s, mc_r, ps_s, ps_r, dt_s, dt_r,
           xs_s, xs_r, rs_s, rs_r, rl_r, so_s, so_r, fo_s, fo_r):
    sec = lax.axis_index("sec")
    row = lax.axis_index("row")
    z, c = row // 2, row % 2
    Z = R // 2
    rows, total = rhs.shape
    W = D.shape[0]
    N = total // 2
    n = N // G
    RZ = 2 * rows

    def rc(src, dst, ss, rs, dsec, drow):
        return pltpu.make_async_remote_copy(
            src_ref=src, dst_ref=dst, send_sem=ss, recv_sem=rs,
            device_id=(dsec, drow), device_id_type=MESH)

    barrier = pltpu.get_barrier_semaphore()

    def signal(dsec, drow):
        pl.semaphore_signal(barrier, inc=1, device_id=(dsec, drow), device_id_type=MESH)

    for k in range(1, R):
        signal(sec, lax.rem(row + k, R))
    for ds in (-1, 1):
        ok = (sec + ds >= 0) & (sec + ds < S)

        @pl.when(ok)
        def _(ds=ds):
            for q in range(Z):
                signal(sec + ds, 2 * q + c)
            signal(sec + ds, 2 * z + 1 - c)

    for k in range(2):
        t = rhs[:, k * N:(k + 1) * N].T.reshape(G, n, rows)
        rT[k] = t
        rTl[k] = t.astype(BF16)

    sides = jnp.where(sec > 0, 1, 0) + jnp.where(sec < S - 1, 1, 0)
    pl.semaphore_wait(barrier, R - 1 + sides * (Z + 1))

    def a0(k):
        to = lax.rem(row + k, R)
        return rc(rTl.at[to % 2], res.at[row], a0_s.at[k], a0_r.at[k], sec, to)

    def rh(k):
        return rc(rT.at[k], rb.at[c], rh_s.at[k], rh_r.at[c], sec - 1, 2 * z + k)

    @pl.when(sec == 0)
    def _():
        for k in range(1, R):
            a0(k).start()
        res[row] = rTl[c]

    @pl.when(sec > 0)
    def _():
        for k in range(2):
            rh(k).start()

    mine = pl.ds(pl.multiple_of(c * rows, rows), rows)

    def ex(t):
        return rc(E.at[t, mine], E.at[t, mine], e_s.at[t], e_r.at[t], sec, 2 * z + 1 - c)

    def make(t, _):
        E[t, mine] = nn(coup[t], D[...]).astype(BF16)
        ex(t).start()
        return 0

    lax.fori_loop(sec + 1, S, make, 0)

    def gathered(g):
        return jnp.concatenate([res[r, g] for r in range(R)], axis=1)

    def mc(s, g, q):
        to = lax.rem(z + q, Z)
        return rc(mco.at[g], res.at[pl.ds(2 * z, 2), g], mc_s.at[g, q], mc_r.at[g, q],
                  s + 1, 2 * to + c)

    def ps(s, t, g):
        return rc(pso.at[t, g], pas.at[t, g], ps_s.at[t, g], ps_r.at[t, g], s + 1, row)

    def xp(s, t, g):
        return rc(xs.at[t, g], xs.at[t, g], xs_s.at[t, g], xs_r.at[t, g], s - 1, row)

    def rsc(s, g, q):
        to = lax.rem(z + q, Z)
        return rc(rso.at[to, g], rsi.at[z, g], rs_s.at[g, q], rs_r.at[g, q],
                  s - 1, 2 * to + c)

    def rlc(g, q):
        to = lax.rem(z + q, Z)
        return rc(rso.at[to, g], rli.at[z, g], rs_s.at[g, q], rl_r.at[g, q], sec, 2 * to + c)

    def dt(s):
        return rc(dto, dti, dt_s, dt_r, s - 1, row)

    def fo():
        return rc(fs.at[1 - c], fb.at[c], fo_s, fo_r, sec, 2 * z + 1 - c)

    def so(slot, dsec, h):
        return rc(sob.at[slot, h], soi.at[c], so_s.at[slot, h], so_r.at[c], dsec, 2 * z + h)

    def own_columns(low):
        if RZ % 128 == 0:
            v = nn(low, D[:, pl.ds(pl.multiple_of(z * RZ, RZ), RZ)])
            return [v[:, :rows], v[:, rows:]]
        v = nn(low, D[...])
        out = [jnp.zeros((low.shape[0], rows), F32) for _ in range(2)]
        for r in range(R):
            out[r % 2] = jnp.where(z == r // 2, v[:, r * rows:(r + 1) * rows], out[r % 2])
        return out

    def section(s):
        last = s == S - 1

        if s == 0:
            for k in range(1, R):
                to = lax.rem(row + R - k, R)
                rc(rTl.at[0], res.at[to], a0_s.at[k], a0_r.at[k], sec, to).wait_recv()
        if not last:
            for k in range(2):
                rc(rT.at[k], rb.at[k], rh_s.at[k], rh_r.at[k], sec, row).wait_recv()
            for t in range(s + 1, S):
                other = pl.ds(pl.multiple_of((1 - c) * rows, rows), rows)
                rc(E.at[t, other], E.at[t, other], e_s.at[t], e_r.at[t], sec, row).wait_recv()

        def forward(g, _):
            if s > 0:
                for q in range(Z):
                    src = lax.rem(z + Z - q, Z)
                    rc(mco.at[g], res.at[pl.ds(2 * src, 2), g], mc_s.at[g, q], mc_r.at[g, q],
                       sec, row).wait_recv()
            x = gathered(g)
            if last:
                y = nt(x, D[...])
                for r in range(R):
                    yb[r, g] = y[:, r * rows:(r + 1) * rows]
                v = own_columns(y.astype(BF16))
                for h in range(2):
                    sob[0, h, g] = v[h]
                    xs[s, g, h] = v[h].astype(BF16)
                xp(s, s, g).start()
                return 0
            for t in range(s + 1, S):
                a = nt(x, E[t])
                if s > 0:
                    ps(s, t, g).wait_recv()
                for h in range(2):
                    ah = a[:, h * rows:(h + 1) * rows]
                    if s > 0:
                        ah = ah + pas[t, g, h].astype(F32)
                    if t == s + 1:
                        mco[g, h] = (rb[h, g] - ah).astype(BF16)
                    else:
                        pso[t, g, h] = ah.astype(BF16)
                if t == s + 1:
                    for q in range(Z):
                        mc(s, g, q).start()
                else:
                    ps(s, t, g).start()
            return 0

        lax.fori_loop(0, G, forward, 0)

        if not last:
            x = jnp.concatenate([res[r].reshape(N, rows) for r in range(R)], axis=1)
            y = nt(x, D[...])
            for r in range(R):
                yb[r] = y[:, r * rows:(r + 1) * rows].reshape(G, n, rows)
            v = own_columns(y.astype(BF16))
            for h in range(2):
                dto[h] = v[h].reshape(G, n, rows)
            if s > 0:
                dt(s).start()
        fs[...] = yb[pl.ds(2 * z, 2)]
        fo().start()
        fb[c] = fs[c]

        if last:
            so(0, s, 1 - c).start()
            soi[c] = sob[0, c]
        else:
            if s < S - 2:
                rc(dto, dti, dt_s, dt_r, sec, row).wait_recv()

            def backward(g, _):
                for t in range(S - 1, s, -1):
                    if t > s + 1 or t == S - 1:
                        xp(s + 1, t, g).wait_recv()
                    else:
                        v = [dti[h, g] for h in range(2)]
                        for q in range(Z):
                            src = lax.rem(z + Z - q, Z)
                            rc(rso.at[0, g], rsi.at[src, g], rs_s.at[g, q], rs_r.at[g, q],
                               sec, row).wait_recv()
                            v = [v[h] - rsi[src, g, h].astype(F32) for h in range(2)]
                        for h in range(2):
                            sob[0, h, g] = v[h]
                            xs[t, g, h] = v[h].astype(BF16)
                    term = nn(jnp.concatenate([xs[t, g, 0], xs[t, g, 1]], axis=1), E[t])
                    p = term if t == S - 1 else p + term
                for r in range(R):
                    rso[r // 2, g, r % 2] = p[:, r * rows:(r + 1) * rows].astype(BF16)
                for q in range(Z):
                    if s > 0:
                        rsc(s, g, q).start()
                    elif q > 0:
                        rlc(g, q).start()
                if s > 0:
                    for t in range(s + 1, S):
                        xp(s, t, g).start()
                return 0

            lax.fori_loop(0, G, backward, 0)
            if s < S - 2:
                for h in range(2):
                    so(0, s + 1, h).start()
            if s == 0:
                def finish(g, _):
                    v = [dto[h, g] - rso[z, g, h].astype(F32) for h in range(2)]
                    for q in range(1, Z):
                        src = lax.rem(z + Z - q, Z)
                        rc(rso.at[0, g], rli.at[src, g], rs_s.at[g, q], rl_r.at[g, q],
                           sec, row).wait_recv()
                        v = [v[h] - rli[src, g, h].astype(F32) for h in range(2)]
                    for h in range(2):
                        sob[1, h, g] = v[h]
                    return 0

                lax.fori_loop(0, G, finish, 0)
                so(1, s, 1 - c).start()
                soi[c] = sob[1, c]

        rc(fs.at[0], fb.at[1 - c], fo_s, fo_r, sec, row).wait_recv()
        fwd[...] = jnp.concatenate([fb[k].reshape(N, rows).T for k in range(2)], axis=1)
        if s == 0 or last:
            rc(sob.at[0, 0], soi.at[1 - c], so_s.at[0, 0], so_r.at[1 - c], sec, row).wait_recv()
        else:
            for k in range(2):
                rc(sob.at[0, 0], soi.at[k], so_s.at[0, 0], so_r.at[k], sec, row).wait_recv()
        sol[...] = jnp.concatenate([soi[k].reshape(N, rows).T for k in range(2)], axis=1)

        if s == 0:
            for k in range(1, R):
                a0(k).wait_send()
        else:
            for k in range(2):
                rh(k).wait_send()
        for t in range(s + 1, S):
            ex(t).wait_send()
        fo().wait_send()
        if 0 < s < S - 1:
            dt(s).wait_send()

        def drain(g, _):
            if not last:
                for q in range(Z):
                    mc(s, g, q).wait_send()
                    if s > 0:
                        rsc(s, g, q).wait_send()
                    elif q > 0:
                        rlc(g, q).wait_send()
                for t in range(s + 2, S):
                    ps(s, t, g).wait_send()
            if s > 0:
                for t in range(min(s + 1, S - 1), S):
                    xp(s, t, g).wait_send()
            return 0

        lax.fori_loop(0, G, drain, 0)
        if last:
            so(0, s, 1 - c).wait_send()
        elif s < S - 2:
            for h in range(2):
                so(0, s + 1, h).wait_send()
        if s == 0:
            so(1, s, 1 - c).wait_send()

    for s in range(S):
        pl.when(sec == s)(functools.partial(section, s))


def local(rhs, coupling, diag_inverse):
    S = lax.axis_size("sec")
    R = lax.axis_size("row")
    rows, total = rhs.shape
    W = diag_inverse.shape[1]
    N = total // 2
    G = GROUPS
    n = N // G
    Z = R // 2
    half = (G, n, rows)
    vm = pltpu.VMEM
    dma = pltpu.SemaphoreType.DMA
    scratch = [
        vm((S, 2 * rows, W), BF16),
        vm((2,) + half, F32),
        vm((2,) + half, BF16),
        vm((2,) + half, F32),
        vm((R,) + half, BF16),
        vm((G, 2, n, rows), BF16),
        vm((S, G, 2, n, rows), BF16),
        vm((S, G, 2, n, rows), BF16),
        vm((R,) + half, F32),
        vm((2,) + half, F32),
        vm((2,) + half, F32),
        vm((2,) + half, F32),
        vm((2,) + half, F32),
        vm((S, G, 2, n, rows), BF16),
        vm((Z, G, 2, n, rows), BF16),
        vm((Z, G, 2, n, rows), BF16),
        vm((Z, G, 2, n, rows), BF16),
        vm((2, 2) + half, F32),
        vm((2,) + half, F32),
        dma((S,)), dma((S,)),
        dma((2,)), dma((2,)),
        dma((R,)), dma((R,)),
        dma((G, Z)), dma((G, Z)),
        dma((S, G)), dma((S, G)),
        dma, dma,
        dma((S, G)), dma((S, G)),
        dma((G, Z)), dma((G, Z)), dma((G, Z)),
        dma((2, 2)), dma((2,)),
        dma, dma,
    ]
    out = jax.ShapeDtypeStruct((rows, total), F32)
    block = pl.BlockSpec(memory_space=pltpu.VMEM)
    return pl.pallas_call(
        functools.partial(kernel, S, R, G),
        out_shape=(out, out),
        in_specs=[block] * 3,
        out_specs=(block, block),
        scratch_shapes=scratch,
        compiler_params=pltpu.CompilerParams(
            collective_id=0, has_side_effects=True, vmem_limit_bytes=48 * 2 ** 20),
    )(rhs, coupling, diag_inverse[0])


def solution(mesh):
    return jax.shard_map(
        local,
        mesh=mesh,
        in_specs=(P(("sec", "row"), None), P(None, "row", "sec"), P("sec", None, None)),
        out_specs=(P(("sec", "row"), None), P(("sec", "row"), None)),
        check_vma=False,
    )
```

time: 421 us -> 62.7 us (0.15)
  waiting for transfers between devices: 248 us -> 0 us
  blocking collectives: 103 us -> 0 us
  Pallas kernels: 0 us -> 56.7 us
  starting transfers between devices: 21.8 us -> 0 us
  other arithmetic: 16 us -> 0 us
  between operations: 13.8 us -> 0.65 us
  matrix products: 11.4 us -> 0 us
    psum x4 -> x0, waiting for transfers between devices: 226 us -> none  [backward_tick(): lax.psum(partial_value.astype(jnp.bfloat16), 'row').astype(jnp.float32)]
    all_gather x8 -> x0, blocking collectives: 103 us -> none  [the longest x4 61.3 us: forward_tick(): whole = lax.all_gather(resid, 'row', axis=0, tiled=True)]
    pallas_call x0 -> x1, Pallas kernels: none -> 56.7 us  [local(): pl.pallas_call(functools.partial(kernel, S, R, G), out_shape=(out, out),...]
    ppermute x4 -> x0, waiting for transfers between devices: 22.1 us -> none  [from_behind(): return lax.ppermute(x, axis, pairs)]
    ppermute x4 -> x0, starting transfers between devices: 21.6 us -> none  [from_behind(): return lax.ppermute(x, axis, pairs)]
    convert_element_type x16 -> x0, other arithmetic: 13.3 us -> none  [the longest x4 8.93 us: backward_tick(): partial_value.astype(jnp.bfloat16)]
    dot_general x6 -> x0, matrix products: 11.4 us -> none  [the longest x3 3.83 us: compute_term(): lax.dot_general(block, incoming, (((0,), (0,)), ((), ())), preferred_elem...]
    unnamed x1 -> x8, local copies, waits for them, and re-layouts: 0.76 us -> 5.02 us
  transfers between devices with their start and end apart: 8 -> 0, of which waited for: 8 -> 0; matrix products, arithmetic and copies ran while one was open for 1% -> 0% of each run, Pallas kernels for 0% -> 0%
where the time goes in v1:
time: 62.7 us; the launch traced here: 62.4 us
  Pallas kernels  56.7 us (90%)
  local copies, waits for them, and re-layouts  5.02 us (8%)
  between operations  0.65 us (1%)
    pallas_call x1, Pallas kernels, local(): pl.pallas_call(functools.partial(kernel, S, R, G), out_shape=(out, out),...  56.7 us
    unnamed x8, local copies, waits for them, and re-layouts  5.02 us

profile of v1, /device:TPU:0, one launch (start us, length us, event | category | flops | bytes accessed | tf_op | source)
XLA Modules:
  0.0 62.4 jit_solution(14643568378654926205)
XLA Ops:
  0.6 0.0 copy-start
  0.6 1.6 %copy-done = bf16[1,1024,1024]{2,1,0:T(8,128)(2,1)S(1)} copy-done((bf16[1,1024,1024]{2,1,0:T(8,128)(2,1)S(1)}, bf16[1,1024,1024]{2,1,0:T(8,128)(2,1)}, u32[]{:S(2)}) %copy-start) | copy-done | bytes 2097176
  2.2 0.0 copy-start.1
  2.2 1.2 %copy-done.1 = bf16[4,128,1024]{2,1,0:T(8,128)(2,1)S(1)} copy-done((bf16[4,128,1024]{2,1,0:T(8,128)(2,1)S(1)}, bf16[4,128,1024]{2,1,0:T(8,128)(2,1)}, u32[]{:S(2)}) %copy-start.1) | copy-done | bytes 1048600
  3.4 0.0 copy-start.2
  3.4 0.9 %copy-done.2 = f32[128,256]{1,0:T(8,128)S(1)} copy-done((f32[128,256]{1,0:T(8,128)S(1)}, f32[128,256]{1,0:T(8,128)}, u32[]{:S(2)}) %copy-start.2) | copy-done | bytes 131096
  4.4 56.7 %shard_map.50 = (f32[128,256]{1,0:T(8,128)S(1)}, f32[128,256]{1,0:T(8,128)S(1)}) custom-call(f32[128,256]{1,0:T(8,128)S(1)} %copy-done.2, bf16[4,128,1024]{2,1,0:T(8,128)(2,1)S(1)} %copy-done.1, bf16[1024,1024]{1,0:T(8,128)(2,1)S(1)} %bitcast.1), custom_call_target="tpu_custom_call" | custom-call | tf_op jit(solution)/shard_map/pallas_call | solution.py:354
  61.1 0.7 %copy.7 = f32[128,256]{1,0:T(8,128)} copy(f32[128,256]{1,0:T(8,128)S(1)} %get-tuple-element.4) | data formatting | bytes 262144
  61.7 0.7 %copy.8 = f32[128,256]{1,0:T(8,128)} copy(f32[128,256]{1,0:T(8,128)S(1)} %get-tuple-element.5) | data formatting | bytes 262144
Async XLA Ops:
  0.6 1.6 %copy-start = (bf16[1,1024,1024]{2,1,0:T(8,128)(2,1)S(1)}, bf16[1,1024,1024]{2,1,0:T(8,128)(2,1)}, u32[]{:S(2)}) copy-start(bf16[1,1024,1024]{2,1,0:T(8,128)(2,1)} %param.5) | copy-start | bytes 6291460
  2.2 1.2 %copy-start.1 = (bf16[4,128,1024]{2,1,0:T(8,128)(2,1)S(1)}, bf16[4,128,1024]{2,1,0:T(8,128)(2,1)}, u32[]{:S(2)}) copy-start(bf16[4,128,1024]{2,1,0:T(8,128)(2,1)} %coup.1) | copy-start | bytes 3145732
  3.4 0.9 %copy-start.2 = (f32[128,256]{1,0:T(8,128)S(1)}, f32[128,256]{1,0:T(8,128)}, u32[]{:S(2)}) copy-start(f32[128,256]{1,0:T(8,128)} %rhs.1) | copy-start | bytes 393220

commit v2 on v1

--- a/solution.py
+++ b/solution.py
@@ -21,10 +21,10 @@
     return jnp.dot(a, b, preferred_element_type=F32)
 
 
-def kernel(S, R, G, rhs, coup, D, sol, fwd,
-           E, rT, rTl, rb, res, mco, pas, pso, yb, fs, fb, dto, dti, xs, rso, rsi, rli, sob, soi,
-           e_s, e_r, rh_s, rh_r, a0_s, a0_r, mc_s, mc_r, ps_s, ps_r, dt_s, dt_r,
-           xs_s, xs_r, rs_s, rs_r, rl_r, so_s, so_r, fo_s, fo_r):
+def kernel(S, R, G, rhs_in, coup_in, D_in, sol, fwd,
+           rhs, coup, D, E, rT, rTl, rb, res, mco, pas, pso, yb, fs, fb, dto, xs, rso, rsi, rli, sob, soi,
+           in_s, e_s, e_r, rh_s, rh_r, a0_s, a0_r, mc_s, mc_r, ps_s, ps_r,
+           xs_s, xs_r, rs_s, rs_r, rl_s, rl_r, so_s, so_r, fo_s, fo_r):
     sec = lax.axis_index("sec")
     row = lax.axis_index("row")
     z, c = row // 2, row % 2
@@ -40,6 +40,13 @@
             src_ref=src, dst_ref=dst, send_sem=ss, recv_sem=rs,
             device_id=(dsec, drow), device_id_type=MESH)
 
+    load_rhs = pltpu.make_async_copy(rhs_in, rhs, in_s.at[0])
+    load_D = pltpu.make_async_copy(D_in, D, in_s.at[1])
+    load_coup = pltpu.make_async_copy(coup_in, coup, in_s.at[2])
+    load_rhs.start()
+    load_D.start()
+    load_coup.start()
+
     barrier = pltpu.get_barrier_semaphore()
 
     def signal(dsec, drow):
@@ -56,6 +63,7 @@
                 signal(sec + ds, 2 * q + c)
             signal(sec + ds, 2 * z + 1 - c)
 
+    load_rhs.wait()
     for k in range(2):
         t = rhs[:, k * N:(k + 1) * N].T.reshape(G, n, rows)
         rT[k] = t
@@ -64,17 +72,21 @@
     sides = jnp.where(sec > 0, 1, 0) + jnp.where(sec < S - 1, 1, 0)
     pl.semaphore_wait(barrier, R - 1 + sides * (Z + 1))
 
-    def a0(k):
+    def a0(g, k):
         to = lax.rem(row + k, R)
-        return rc(rTl.at[to % 2], res.at[row], a0_s.at[k], a0_r.at[k], sec, to)
+        return rc(rTl.at[to % 2, g], res.at[row, g], a0_s.at[g, k], a0_r.at[g, k], sec, to)
 
     def rh(k):
         return rc(rT.at[k], rb.at[c], rh_s.at[k], rh_r.at[c], sec - 1, 2 * z + k)
 
     @pl.when(sec == 0)
     def _():
-        for k in range(1, R):
-            a0(k).start()
+        def send(g, _):
+            for k in range(1, R):
+                a0(g, k).start()
+            return 0
+
+        lax.fori_loop(0, G, send, 0)
         res[row] = rTl[c]
 
     @pl.when(sec > 0)
@@ -92,6 +104,8 @@
         ex(t).start()
         return 0
 
+    load_D.wait()
+    load_coup.wait()
     lax.fori_loop(sec + 1, S, make, 0)
 
     def gathered(g):
@@ -113,18 +127,16 @@
         return rc(rso.at[to, g], rsi.at[z, g], rs_s.at[g, q], rs_r.at[g, q],
                   s - 1, 2 * to + c)
 
-    def rlc(g, q):
-        to = lax.rem(z + q, Z)
-        return rc(rso.at[to, g], rli.at[z, g], rs_s.at[g, q], rl_r.at[g, q], sec, 2 * to + c)
-
-    def dt(s):
-        return rc(dto, dti, dt_s, dt_r, s - 1, row)
+    def rlc(g, k):
+        to = lax.rem(row + k, R)
+        return rc(rso.at[to // 2, g, to % 2], rli.at[z, c, g], rl_s.at[g, k], rl_r.at[g, k],
+                  sec, to)
 
     def fo():
         return rc(fs.at[1 - c], fb.at[c], fo_s, fo_r, sec, 2 * z + 1 - c)
 
-    def so(slot, dsec, h):
-        return rc(sob.at[slot, h], soi.at[c], so_s.at[slot, h], so_r.at[c], dsec, 2 * z + h)
+    def so(slot, dsec, h, g):
+        return rc(sob.at[slot, h, g], soi.at[c, g], so_s.at[h, g], so_r.at[c, g], dsec, 2 * z + h)
 
     def own_columns(low):
         if RZ % 128 == 0:
@@ -136,25 +148,28 @@
             out[r % 2] = jnp.where(z == r // 2, v[:, r * rows:(r + 1) * rows], out[r % 2])
         return out
 
+    def arrived(t):
+        other = pl.ds(pl.multiple_of((1 - c) * rows, rows), rows)
+        rc(E.at[t, other], E.at[t, other], e_s.at[t], e_r.at[t], sec, row).wait_recv()
+
     def section(s):
         last = s == S - 1
 
-        if s == 0:
-            for k in range(1, R):
-                to = lax.rem(row + R - k, R)
-                rc(rTl.at[0], res.at[to], a0_s.at[k], a0_r.at[k], sec, to).wait_recv()
         if not last:
             for k in range(2):
                 rc(rT.at[k], rb.at[k], rh_s.at[k], rh_r.at[k], sec, row).wait_recv()
-            for t in range(s + 1, S):
-                other = pl.ds(pl.multiple_of((1 - c) * rows, rows), rows)
-                rc(E.at[t, other], E.at[t, other], e_s.at[t], e_r.at[t], sec, row).wait_recv()
+            arrived(s + 1)
 
         def forward(g, _):
             if s > 0:
                 for q in range(Z):
                     src = lax.rem(z + Z - q, Z)
                     rc(mco.at[g], res.at[pl.ds(2 * src, 2), g], mc_s.at[g, q], mc_r.at[g, q],
+                       sec, row).wait_recv()
+            else:
+                for k in range(1, R):
+                    src = lax.rem(row + R - k, R)
+                    rc(rTl.at[0, g], res.at[src, g], a0_s.at[g, k], a0_r.at[g, k],
                        sec, row).wait_recv()
             x = gathered(g)
             if last:
@@ -166,8 +181,12 @@
                     sob[0, h, g] = v[h]
                     xs[s, g, h] = v[h].astype(BF16)
                 xp(s, s, g).start()
+                so(0, s, 1 - c, g).start()
+                soi[c, g] = sob[0, c, g]
                 return 0
             for t in range(s + 1, S):
+                if t > s + 1:
+                    pl.when(g == 0)(functools.partial(arrived, t))
                 a = nt(x, E[t])
                 if s > 0:
                     ps(s, t, g).wait_recv()
@@ -196,25 +215,17 @@
             v = own_columns(y.astype(BF16))
             for h in range(2):
                 dto[h] = v[h].reshape(G, n, rows)
-            if s > 0:
-                dt(s).start()
         fs[...] = yb[pl.ds(2 * z, 2)]
         fo().start()
         fb[c] = fs[c]
 
-        if last:
-            so(0, s, 1 - c).start()
-            soi[c] = sob[0, c]
-        else:
-            if s < S - 2:
-                rc(dto, dti, dt_s, dt_r, sec, row).wait_recv()
-
+        if not last:
             def backward(g, _):
                 for t in range(S - 1, s, -1):
                     if t > s + 1 or t == S - 1:
                         xp(s + 1, t, g).wait_recv()
                     else:
-                        v = [dti[h, g] for h in range(2)]
+                        v = [jnp.zeros((n, rows), F32) for h in range(2)]
                         for q in range(Z):
                             src = lax.rem(z + Z - q, Z)
                             rc(rso.at[0, g], rsi.at[src, g], rs_s.at[g, q], rs_r.at[g, q],
@@ -226,57 +237,68 @@
                     term = nn(jnp.concatenate([xs[t, g, 0], xs[t, g, 1]], axis=1), E[t])
                     p = term if t == S - 1 else p + term
                 for r in range(R):
-                    rso[r // 2, g, r % 2] = p[:, r * rows:(r + 1) * rows].astype(BF16)
-                for q in range(Z):
-                    if s > 0:
+                    own = jnp.where(z == r // 2, dto[r % 2, g], 0.0)
+                    rso[r // 2, g, r % 2] = (p[:, r * rows:(r + 1) * rows] - own).astype(BF16)
+                if s == 0:
+                    for k in range(1, R):
+                        rlc(g, k).start()
+                    rli[z, c, g] = rso[z, g, c]
+                else:
+                    for q in range(Z):
                         rsc(s, g, q).start()
-                    elif q > 0:
-                        rlc(g, q).start()
-                if s > 0:
                     for t in range(s + 1, S):
                         xp(s, t, g).start()
+                if s < S - 2:
+                    for h in range(2):
+                        so(0, s + 1, h, g).start()
                 return 0
 
             lax.fori_loop(0, G, backward, 0)
-            if s < S - 2:
-                for h in range(2):
-                    so(0, s + 1, h).start()
             if s == 0:
                 def finish(g, _):
-                    v = [dto[h, g] - rso[z, g, h].astype(F32) for h in range(2)]
-                    for q in range(1, Z):
-                        src = lax.rem(z + Z - q, Z)
-                        rc(rso.at[0, g], rli.at[src, g], rs_s.at[g, q], rl_r.at[g, q],
-                           sec, row).wait_recv()
-                        v = [v[h] - rli[src, g, h].astype(F32) for h in range(2)]
-                    for h in range(2):
-                        sob[1, h, g] = v[h]
+                    for k in range(1, R):
+                        src = lax.rem(row + R - k, R)
+                        rc(rso.at[0, g, 0], rli.at[src // 2, src % 2, g], rl_s.at[g, k],
+                           rl_r.at[g, k], sec, row).wait_recv()
+                    for k in range(2):
+                        v = jnp.zeros((n, rows), F32)
+                        for q in range(Z):
+                            v = v - rli[q, k, g].astype(F32)
+                        soi[k, g] = v
                     return 0
 
                 lax.fori_loop(0, G, finish, 0)
-                so(1, s, 1 - c).start()
-                soi[c] = sob[1, c]
 
         rc(fs.at[0], fb.at[1 - c], fo_s, fo_r, sec, row).wait_recv()
         fwd[...] = jnp.concatenate([fb[k].reshape(N, rows).T for k in range(2)], axis=1)
-        if s == 0 or last:
-            rc(sob.at[0, 0], soi.at[1 - c], so_s.at[0, 0], so_r.at[1 - c], sec, row).wait_recv()
-        else:
-            for k in range(2):
-                rc(sob.at[0, 0], soi.at[k], so_s.at[0, 0], so_r.at[k], sec, row).wait_recv()
+        if s > 0:
+            def collect(g, _):
+                for k in range(2):
+                    if not last:
+                        rc(sob.at[0, 0, g], soi.at[k, g], so_s.at[0, g], so_r.at[k, g],
+                           sec, row).wait_recv()
+                if last:
+                    rc(sob.at[0, 0, g], soi.at[1 - c, g], so_s.at[0, g], so_r.at[1 - c, g],
+                       sec, row).wait_recv()
+                return 0
+
+            lax.fori_loop(0, G, collect, 0)
         sol[...] = jnp.concatenate([soi[k].reshape(N, rows).T for k in range(2)], axis=1)
 
         if s == 0:
-            for k in range(1, R):
-                a0(k).wait_send()
+            def drain_first(g, _):
+                for k in range(1, R):
+                    a0(g, k).wait_send()
+                    rlc(g, k).wait_send()
+                return 0
+
+            lax.fori_loop(0, G, drain_first, 0)
         else:
             for k in range(2):
                 rh(k).wait_send()
         for t in range(s + 1, S):
             ex(t).wait_send()
         fo().wait_send()
-        if 0 < s < S - 1:
-            dt(s).wait_send()
 
         def drain(g, _):
             if not last:
@@ -284,23 +306,19 @@
                     mc(s, g, q).wait_send()
                     if s > 0:
                         rsc(s, g, q).wait_send()
-                    elif q > 0:
-                        rlc(g, q).wait_send()
                 for t in range(s + 2, S):
                     ps(s, t, g).wait_send()
             if s > 0:
                 for t in range(min(s + 1, S - 1), S):
                     xp(s, t, g).wait_send()
+            if last:
+                so(0, s, 1 - c, g).wait_send()
+            elif s < S - 2:
+                for h in range(2):
+                    so(0, s + 1, h, g).wait_send()
             return 0
 
         lax.fori_loop(0, G, drain, 0)
-        if last:
-            so(0, s, 1 - c).wait_send()
-        elif s < S - 2:
-            for h in range(2):
-                so(0, s + 1, h).wait_send()
-        if s == 0:
-            so(1, s, 1 - c).wait_send()
 
     for s in range(S):
         pl.when(sec == s)(functools.partial(section, s))
@@ -319,6 +337,9 @@
     vm = pltpu.VMEM
     dma = pltpu.SemaphoreType.DMA
     scratch = [
+        vm((rows, total), F32),
+        vm(coupling.shape, BF16),
+        vm((W, W), BF16),
         vm((S, 2 * rows, W), BF16),
         vm((2,) + half, F32),
         vm((2,) + half, BF16),
@@ -331,22 +352,21 @@
         vm((2,) + half, F32),
         vm((2,) + half, F32),
         vm((2,) + half, F32),
-        vm((2,) + half, F32),
         vm((S, G, 2, n, rows), BF16),
         vm((Z, G, 2, n, rows), BF16),
         vm((Z, G, 2, n, rows), BF16),
-        vm((Z, G, 2, n, rows), BF16),
-        vm((2, 2) + half, F32),
-        vm((2,) + half, F32),
-        dma((S,)), dma((S,)),
+        vm((Z, 2) + half, BF16),
+        vm((1, 2) + half, F32),
+        vm((2,) + half, F32),
+        dma((3,)), dma((S,)), dma((S,)),
         dma((2,)), dma((2,)),
-        dma((R,)), dma((R,)),
+        dma((G, R)), dma((G, R)),
         dma((G, Z)), dma((G, Z)),
         dma((S, G)), dma((S, G)),
-        dma, dma,
         dma((S, G)), dma((S, G)),
-        dma((G, Z)), dma((G, Z)), dma((G, Z)),
-        dma((2, 2)), dma((2,)),
+        dma((G, Z)), dma((G, Z)),
+        dma((G, R)), dma((G, R)),
+        dma((2, G)), dma((2, G)),
         dma, dma,
     ]
     out = jax.ShapeDtypeStruct((rows, total), F32)
@@ -354,11 +374,11 @@
     return pl.pallas_call(
         functools.partial(kernel, S, R, G),
         out_shape=(out, out),
-        in_specs=[block] * 3,
+        in_specs=[pl.BlockSpec(memory_space=pltpu.HBM)] * 3,
         out_specs=(block, block),
         scratch_shapes=scratch,
         compiler_params=pltpu.CompilerParams(
-            collective_id=0, has_side_effects=True, vmem_limit_bytes=48 * 2 ** 20),
+            collective_id=0, has_side_effects=True, vmem_limit_bytes=127 * 2 ** 19),
     )(rhs, coupling, diag_inverse[0])
 
 

time: 62.7 us -> 57 us (0.909)
  Pallas kernels: 56.7 us -> 53 us
  local copies, waits for them, and re-layouts: 5.02 us -> 3.14 us
    pallas_call x1, Pallas kernels: 56.7 us -> 53 us  [local(): pl.pallas_call(functools.partial(kernel, S, R, G), out_shape=(out, out),...]
    unnamed x8 -> x2, local copies, waits for them, and re-layouts: 5.02 us -> 3.14 us
where the time goes in v2:
time: 57 us; the launch traced here: 56.8 us
  Pallas kernels  53 us (93%)
  local copies, waits for them, and re-layouts  3.14 us (6%)
  between operations  0.64 us (1%)
    pallas_call x1, Pallas kernels, local(): pl.pallas_call(functools.partial(kernel, S, R, G), out_shape=(out, out),...  53 us
    unnamed x2, local copies, waits for them, and re-layouts  3.14 us

profile of v2, /device:TPU:0, one launch (start us, length us, event | category | flops | bytes accessed | tf_op | source)
XLA Modules:
  0.0 56.8 jit_solution(2924806175339723676)
XLA Ops:
  0.6 53.0 %shard_map.50 = (f32[128,256]{1,0:T(8,128)}, f32[128,256]{1,0:T(8,128)}) custom-call(f32[128,256]{1,0:T(8,128)} %rhs_in.1, bf16[4,128,1024]{2,1,0:T(8,128)(2,1)} %coup_in.1, bf16[1024,1024]{1,0:T(8,128)(2,1)} %bitcast.1), custom_call_target="tpu_custom_call" | custom-call | tf_op jit(solution)/shard_map/pallas_call | solution.py:374
  53.7 1.6 %copy.7 = f32[128,256]{1,0:T(8,128)} copy(f32[128,256]{1,0:T(8,128)} %get-tuple-element.4) | data formatting | bytes 262144
  55.2 1.6 %copy.8 = f32[128,256]{1,0:T(8,128)} copy(f32[128,256]{1,0:T(8,128)} %get-tuple-element.5) | data formatting | bytes 262144
